TPU v7x, 32 devices: a whole 2x2x4 slice. The times are simulated.
32 devices in a mesh: sub: 8 (over y, x, core), grp: 4 (over z).
Axes of the slice: x: 2, y: 2, z: 4, core: 2. Of those that a mesh axis runs over, the one named last changes fastest.
Arguments:
- phi: bfloat16 [64, 400, 2048], P('sub', 'grp'), may hold values from -0.5 to 0.5
- psi: bfloat16 [64, 400, 2048], P('sub', 'grp'), may hold values from -1.25 to 1.25
- k_blocks: bfloat16 [64, 24, 128, 128], P('sub'), may hold values from -0.5 to 0.5
- m_blocks: bfloat16 [64, 24, 128, 128], P('sub'), may hold values from -0.5 to 0.5
- block_row: int32 [64, 24], P('sub'), may hold values from 0 to 15
- block_col: int32 [64, 24], P('sub'), may hold values from 0 to 31
- live: int32 [64], P('sub'), may hold values from 1 to 24, 768 in all
Outputs:
- grid_k: float32 [8, 4, 8, 100, 800], P('sub', 'grp')
- grid_m: float32 [8, 4, 8, 100, 800], P('sub', 'grp')
Inputs may be any that keep to these rules, and one draw needn't show every extreme that they name: Slots n >= live[i] are not part of substructure i's pattern; the largest count is 24. `block_row`: several used slots may name the same block position; their terms add. `block_col`: blocks below 16 lie on the left interface, the others on the right one.
All inputs are finite; a program needn't handle non-finite values. No bound on the sum of `live` on one device may be relied on, other than what follows from the above.
Results may differ from a plain program's by a relative error of at most 0.0029.
Values may be sent and summed in bfloat16 or wider, within the bound.
No kernel may reach another device: no remote copies, remote signals or barrier semaphores. Data moves between devices by JAX's collectives and lax.ppermute only.
A program may use at most 256 MiB of HBM per device.

v0:
```python
import functools

import jax
import jax.numpy as jnp
from jax import lax
from jax.experimental import pallas as pl
from jax.experimental.pallas import tpu as pltpu
from jax.sharding import PartitionSpec as P

EDGE = 128
ROWS = 112
SLOTS = 8
BITE = 4
ROOM = 94
PHI_ROOM = 92
MORE = 16
MIB = 1 << 20
LIGHT = pl.CostEstimate(flops=1, bytes_accessed=1, transcendentals=0)
HEAVY = pl.CostEstimate(flops=25_000_000_000, bytes_accessed=1, transcendentals=0)


def up_to(limit, body, unroll=1):
    lax.fori_loop(0, limit, lambda n, _: (body(n), 0)[1], 0, unroll=unroll)


def by_four(limit, body):
    def four(step):
        for k in range(4):
            body(jnp.minimum(step * 4 + k, limit - 1))

    up_to((limit + 3) // 4, four)


def lanes(block, count=1):
    return pl.ds(pl.multiple_of(block * EDGE, EDGE), count * EDGE)


class Meta:
    def __init__(self, count, slots, blocks_per):
        self.count, self.slots, self.blocks_per = count, slots, blocks_per
        self.keys = (count + 1) * blocks_per
        self.order = 0
        self.start = self.keys + max(ROOM + MORE, 2 * PHI_ROOM)
        self.size = self.start + count + 2


def list_kernel(at, shift, live, block, meta, *refs):
    (*places, flags) = refs

    def clear(n):
        flags[n] = 0

    up_to(at.keys, clear, unroll=16)
    for i in range(at.count):

        def mark(n, i=i):
            flags[block[i, n] + (i + shift) * at.blocks_per] = 1

        up_to(live[i], mark)

    def place(key, taken):
        needed = flags[key]
        meta[at.order + taken] = key
        flags[key] = taken
        return taken + needed

    taken = 0
    for side in range(at.count + 1):
        meta[at.start + side] = taken
        taken = lax.fori_loop(
            side * at.blocks_per, (side + 1) * at.blocks_per, place, taken, unroll=at.blocks_per
        )
    meta[at.start + at.count + 1] = taken

    for found in places:
        for i in range(at.count):

            def find(n, i=i, found=found):
                found[i, n] = flags[block[i, n] + (i + shift) * at.blocks_per]

            up_to(live[i], find)


def listed(at, shift, block, live, with_places=False):
    out = [jax.ShapeDtypeStruct((at.size,), jnp.int32)]
    if with_places:
        out.append(jax.ShapeDtypeStruct(block.shape, jnp.int32))
    return pl.pallas_call(
        functools.partial(list_kernel, at, shift),
        out_shape=out,
        in_specs=[pl.BlockSpec(memory_space=pltpu.SMEM)] * 2,
        out_specs=[pl.BlockSpec(memory_space=pltpu.SMEM)] * len(out),
        scratch_shapes=[pltpu.SMEM((at.keys,), jnp.int32)],
        cost_estimate=LIGHT,
    )(live, block)


def pack_kernel(at, first, room, meta, *refs):
    borders, psi, out = refs[:-2], refs[-2], refs[-1]
    split = jnp.clip(meta[at.start + 1] - first, 0, room)
    end = jnp.clip(meta[at.start + at.count + 1] - first, 0, room)

    def from_border(c):
        for border in borders:
            out[:, lanes(c)] = border[:, lanes(meta[at.order + first + c])]

    def from_psi(c):
        key = meta[at.order + first + c]
        out[:, lanes(c)] = psi[key // at.blocks_per - 1, :, lanes(key % at.blocks_per)]

    def from_none(c):
        out[:, lanes(c)] = jnp.zeros((out.shape[0], EDGE), out.dtype)

    up_to(split, from_border)
    up_to(end - split, lambda c: from_psi(split + c))
    up_to(room - end, lambda c: from_none(end + c))


def pack(at, first, room, meta, psi, *borders):
    return pl.pallas_call(
        functools.partial(pack_kernel, at, first, room),
        out_shape=jax.ShapeDtypeStruct((psi.shape[1], room * EDGE), psi.dtype),
        in_specs=[pl.BlockSpec(memory_space=pltpu.SMEM)]
        + [pl.BlockSpec(memory_space=pltpu.VMEM)] * (1 + len(borders)),
        out_specs=pl.BlockSpec(memory_space=pltpu.VMEM),
        compiler_params=pltpu.CompilerParams(vmem_limit_bytes=8 * MIB),
        cost_estimate=LIGHT,
    )(meta, *borders, psi)


def coupling_kernel(at, room, many, meta, live, row, col, *refs):
    phis, (k_blocks, m_blocks, out, total) = refs[:many], refs[many:]
    i = pl.program_id(0)
    couple_one(at, room, i, meta, live, row, col, phis, k_blocks, m_blocks, out, total)


def couple_one(at, room, i, meta, live, row, col, phis, k_blocks, m_blocks, out, total):
    modes, blocks = phis[0].shape[1], phis[0].shape[2] // EDGE
    here, middle, end = (meta[at.start + i + n] for n in range(3))
    first = at.blocks_per * i

    def clear(n):
        total[meta[at.order + here + n] - first] = jnp.zeros(total.shape[1:], total.dtype)

    by_four(end - here, clear)

    def add_slots(step):
        terms = []
        for n in range(SLOTS):
            slot = jnp.minimum(step * SLOTS + n, at.slots - 1)
            where = row[i, slot]
            here = (step * SLOTS + n < live[i]) & (where >= 0) & (where < blocks)
            which = lanes(jnp.clip(where, 0, blocks - 1))
            picked = sum([phi[0, :, which] for phi in phis[1:]], phis[0][0, :, which])
            both = jnp.concatenate([k_blocks[0, slot], m_blocks[0, slot]], axis=1)
            to = jnp.where(here, col[i, slot], 2 * at.blocks_per)
            terms.append((to, jnp.dot(picked, both, preferred_element_type=jnp.float32)))
        for to, term in terms:
            total[to] += term

    up_to((live[i] + SLOTS - 1) // SLOTS, add_slots)

    def put(flavour, c):
        done = total[meta[at.order + c] - first].astype(out.dtype)
        out[flavour * ROWS : flavour * ROWS + modes, lanes(c)] = done[:, :EDGE]
        out[(flavour + 1) * ROWS : (flavour + 1) * ROWS + modes, lanes(c)] = done[:, EDGE:]

    def blank(top, c):
        out[top : top + 2 * ROWS, lanes(c)] = jnp.zeros((2 * ROWS, EDGE), out.dtype)

    by_four(middle - here, lambda n: put(2, here + n))
    by_four(end - middle, lambda n: put(0, middle + n))

    @pl.when(i == 0)
    def _():
        up_to(middle, lambda n: blank(0, n))

    @pl.when(i == at.count - 1)
    def _():
        up_to(room - middle, lambda n: blank(2 * ROWS, middle + n))
        up_to(room - end, lambda n: blank(0, end + n))


def couple(at, room, meta, live, row, col, phis, k_blocks, m_blocks, cost=LIGHT):
    _, modes, width = phis[0].shape
    count, slots = k_blocks.shape[:2]
    return pl.pallas_call(
        functools.partial(coupling_kernel, at, room, len(phis)),
        out_shape=jax.ShapeDtypeStruct((4 * ROWS, room * EDGE), phis[0].dtype),
        grid_spec=pltpu.PrefetchScalarGridSpec(
            num_scalar_prefetch=4,
            grid=(count,),
            in_specs=[
                pl.BlockSpec(
                    (1, modes, width), lambda i, *_, phi=phi: (0 if phi.shape[0] == 1 else i, 0, 0)
                )
                for phi in phis
            ]
            + [pl.BlockSpec((1, slots, EDGE, EDGE), lambda i, *_: (i, 0, 0, 0))] * 2,
            out_specs=pl.BlockSpec(
                (4 * ROWS, room * EDGE), lambda i, *_: (0, 0), pipeline_mode=pl.Buffered(1)
            ),
            scratch_shapes=[pltpu.VMEM((2 * at.blocks_per + 1, modes, 2 * EDGE), jnp.float32)],
        ),
        compiler_params=pltpu.CompilerParams(vmem_limit_bytes=56 * MIB),
        cost_estimate=cost,
    )(meta, live, row, col, *phis, k_blocks, m_blocks)


def sum_blocks(at, meta, bounds, couplings, shard, groups, right, totals):
    low, high = bounds
    modes = shard.shape[1]

    def on_side(side):
        begin = jnp.maximum(meta[at.start + side], low)
        end = jnp.minimum(meta[at.start + side + 1], high)

        def bite(n):
            want = begin + n * BITE
            first = jnp.minimum(want, high - BITE)
            lane = lax.broadcasted_iota(jnp.int32, (modes, BITE * EDGE), 1) + first * EDGE
            inside = (lane >= want * EDGE) & (lane < end * EDGE)
            for g, group in enumerate(groups):
                part = shard[group[0], :, lanes(first, BITE)]
                for other in group[1:]:
                    part = part + shard[other, :, lanes(first, BITE)]
                part = jnp.where(inside, part, jnp.zeros_like(part))
                right[g * EDGE : g * EDGE + modes, :] = part
            for coupling, total in zip(couplings, totals):
                total[side] += lax.dot_general(
                    coupling[:, lanes(first, BITE)],
                    right[...],
                    (((1,), (1,)), ((), ())),
                    preferred_element_type=jnp.float32,
                )

        up_to(jnp.maximum(end - begin + BITE - 1, 0) // BITE, bite)

    up_to(at.count + 1, on_side)


def put_products(at, groups, modes, total, out):
    for side in range(at.count + 1):
        for g in range(len(groups)):
            for flavour, (sub, part) in enumerate(
                ((side - 1, 1), (side - 1, 3), (side, 0), (side, 2))
            ):
                if 0 <= sub < at.count:
                    top, to = flavour * ROWS, (g * 4 + part) * modes
                    one = total[side, top : top + modes, g * EDGE : g * EDGE + modes]
                    out[sub, :modes, to : to + modes] = one.astype(out.dtype)


def grouped(sets):
    groups, taken = [], 0
    for size in sets:
        groups.append(range(taken, taken + size))
        taken += size
    return groups


def put_spread(at, modes, me, total, outs):
    for k, out in enumerate(outs):
        sub = jnp.bitwise_xor(me, k)
        for part, (side, flavour) in enumerate(((sub, 2), (sub + 1, 0), (sub, 3), (sub + 1, 1))):
            one = total[side, flavour * ROWS : flavour * ROWS + modes, :modes]
            out[:modes, part * modes : (part + 1) * modes] = one.astype(out.dtype)


def project_kernel(at, room, sets, many, spread, meta, me, *refs):
    couplings, refs = refs[:many], refs[many:]
    shards, refs = refs[: sum(sets)], refs[sum(sets) :]
    pieces = at.count if spread else 0
    outs, spreads, refs = refs[:many], refs[many - 1 : many - 1 + pieces], refs[many + max(pieces - 1, 0) :]
    helds, totals, (shard, right, held_done, shard_done) = refs[:many], refs[many : 2 * many], refs[2 * many :]
    parts = [(0, room // 2), (room // 2, room)]
    coming = [[], []]
    for k, one in enumerate(shards):
        coming[0].append(pltpu.make_async_copy(one, shard.at[k], shard_done.at[k]))
    for n, (low, high) in enumerate(parts):
        to = pl.ds(low * EDGE, (high - low) * EDGE)
        for k, (coupling, held) in enumerate(zip(couplings, helds)):
            coming[n].append(
                pltpu.make_async_copy(coupling.at[:, to], held.at[:, to], held_done.at[2 * k + n])
            )
    for copy in coming[0] + coming[1]:
        copy.start()
    right[...] = jnp.zeros(right.shape, right.dtype)
    for total in totals:
        total[...] = jnp.zeros(total.shape, total.dtype)
    for bounds, here in zip(parts, coming):
        for copy in here:
            copy.wait()
        sum_blocks(at, meta, bounds, helds, shard, grouped(sets), right, totals)
    for n, (total, out) in enumerate(zip(totals, outs)):
        if spread and n == many - 1:
            put_spread(at, shard.shape[1], me[0], total, spreads)
        else:
            put_products(at, grouped(sets), shard.shape[1], total, out)


def project(at, meta, couplings, groups, spread=False):
    flat = [shard for group in groups for shard in group]
    modes, held = flat[0].shape[0], couplings[0]
    sets = tuple(len(group) for group in groups)
    n, many, room = len(groups), len(couplings), held.shape[1] // EDGE
    wide = -(-n * 4 * modes // EDGE) * EDGE
    tall = -(-modes // 8) * 8
    out = [jax.ShapeDtypeStruct((at.count, tall, wide), held.dtype)] * many
    if spread:
        out = out[:-1] + [jax.ShapeDtypeStruct((tall, wide), held.dtype)] * at.count
    me = lax.axis_index("sub").astype(jnp.int32)[None]
    return pl.pallas_call(
        functools.partial(project_kernel, at, room, sets, many, spread),
        out_shape=out,
        in_specs=[pl.BlockSpec(memory_space=pltpu.SMEM)] * 2
        + [pl.BlockSpec(memory_space=pltpu.HBM)] * (many + len(flat)),
        out_specs=[pl.BlockSpec(memory_space=pltpu.VMEM)] * len(out),
        scratch_shapes=[pltpu.VMEM(held.shape, held.dtype)] * many
        + [pltpu.VMEM((at.count + 1, 4 * ROWS, n * EDGE), jnp.float32)] * many
        + [
            pltpu.VMEM((len(flat), modes, held.shape[1]), held.dtype),
            pltpu.VMEM((n * EDGE, BITE * EDGE), held.dtype),
            pltpu.SemaphoreType.DMA((2 * many,)),
            pltpu.SemaphoreType.DMA((len(flat),)),
        ],
        compiler_params=pltpu.CompilerParams(vmem_limit_bytes=56 * MIB),
        cost_estimate=LIGHT,
    )(meta, me, *couplings, *flat)


def couple_end(at, meta, ints, places, phi_in, blocks):
    live, _, col = ints
    phis = [one[None] for one in phi_in]
    return couple(at, ROOM, meta, live, places, col, phis, *blocks, cost=HEAVY)


def assemble_kernel(modes, place, near, second, *refs):
    rows = refs[-2].shape[1]
    thirds, (grid_k, grid_m, wide, sorted_third) = refs[:-4], refs[-4:]
    third = thirds[0]
    if len(thirds) > 1:
        third = sorted_third
        for k, one in enumerate(thirds):
            third[jnp.bitwise_xor(place[1], k)] = one[...]
    own, left, right = ((near, g * 4 * modes) for g in range(3))
    second, third = (second, 0), (third, 0)
    plans = (
        (own, right, second, third),
        (left, own, right, second),
        (second, left, own, right),
        (third, second, left, own),
    )
    for which, grid in enumerate((grid_k, grid_m)):
        for z, plan in enumerate(plans):

            @pl.when(place[0] == z)
            def _(plan=plan, which=which):
                for far in range(2):
                    for h, (part, base) in enumerate(plan):
                        take = base + (2 * which + far) * modes
                        at = (4 * far + h) * modes
                        wide[:, :, at : at + modes] = part[:, :rows, take : take + modes].astype(
                            jnp.float32
                        )

        grid[...] = jnp.transpose(wide[...], (1, 0, 2))


def assemble(place, parts, thirds, modes, rows):
    owners = parts[0].shape[0]
    out = jax.ShapeDtypeStruct((rows, owners, 8 * modes), jnp.float32)
    group = min(owners, 8)
    block = pl.BlockSpec((rows, group, 8 * modes), lambda d, place: (0, d, 0))

    def taken(part):
        if len(part.shape) == 2:
            return pl.BlockSpec(part.shape, lambda d, place: (0, 0))
        return pl.BlockSpec((group, *part.shape[1:]), lambda d, place: (d, 0, 0))

    return pl.pallas_call(
        functools.partial(assemble_kernel, modes),
        out_shape=[out, out],
        grid_spec=pltpu.PrefetchScalarGridSpec(
            num_scalar_prefetch=1,
            grid=(owners // group,),
            in_specs=[taken(part) for part in (*parts, *thirds)],
            out_specs=[block] * 2,
            scratch_shapes=[
                pltpu.VMEM((group, rows, 8 * modes), jnp.float32),
                pltpu.VMEM((group, *thirds[0].shape[-2:]), thirds[0].dtype),
            ],
        ),
        compiler_params=pltpu.CompilerParams(vmem_limit_bytes=56 * MIB),
        cost_estimate=LIGHT,
    )(place, *parts, *thirds)


def moved(shard, axis, by, sources=None):
    length = lax.axis_size(axis)
    sources = range(length) if sources is None else sources
    pairs = [(i, i + by) for i in sources if 0 <= i + by < length]
    return lax.ppermute(shard, axis, pairs)


def to_owners(part, modes):
    count, _, cols = part.shape
    owners = lax.axis_size("sub")
    if owners != count:
        part = part[:, :modes].reshape(owners, count * modes // owners, cols)
    return lax.all_to_all(part, "sub", split_axis=0, concat_axis=0, tiled=True)


def sent_in(phi_packed):
    last = lax.axis_size("grp") - 1
    return moved(phi_packed, "grp", 1, [0]), moved(phi_packed, "grp", -1, [last])


def sent_back(part):
    last = lax.axis_size("grp") - 1
    return lax.ppermute(part, "grp", [(1, 0), (last - 1, last)])


def sent_to_owners(parts):
    last, owners = lax.axis_size("grp") - 1, lax.axis_size("sub")
    moved_to = []
    for k, part in enumerate(parts):
        pairs = []
        for source, target in ((1, 0), (last - 1, last)):
            for sub in range(owners):
                pairs.append((sub * (last + 1) + source, (sub ^ k) * (last + 1) + target))
        moved_to.append(lax.ppermute(part, ("sub", "grp"), pairs))
    return moved_to


def both_ways(left, right):
    return moved(left, "grp", 1), moved(right, "grp", -1)


def main_path(at, lists, ints, phi, psi, border, blocks):
    meta, phi_meta, places, beside = lists
    modes = phi.shape[1]
    hold = lax.optimization_barrier

    own = pack(at, 0, ROOM, meta, psi, border)
    one = both_ways(own, own)
    own, phi, phi_meta = hold((own, phi, phi_meta))
    coupling = couple(at, ROOM, meta, *ints, [phi], *blocks)
    phi_in = sent_in(pack(at, 0, PHI_ROOM, phi_meta, phi))
    one, coupling, beside = hold((one, coupling, beside))
    last = lax.axis_size("grp") - 1
    two = (
        moved(one[0], "grp", 1, range(1, last)),
        moved(one[1], "grp", -1, range(last - 1, 0, -1)),
    )
    (near,) = project(at, meta, [coupling], [(own,), (one[0],), (one[1],)])
    near = to_owners(near, modes)
    end = couple_end(at, meta, ints, places, phi_in, blocks)
    two, near, end = hold((two, near, end))
    direct = lax.axis_size("sub") == phi.shape[0]
    second, *third = project(at, meta, [coupling, end], [two], spread=direct)
    third = sent_to_owners(third) if direct else [sent_back(third[0])]
    second = to_owners(second, modes)
    if not direct:
        third, second, near = hold((third, second, near))
        third = [to_owners(third[0], modes)]
    place = jnp.stack([lax.axis_index("grp"), lax.axis_index("sub")]).astype(jnp.int32)
    rows = phi.shape[0] * modes // lax.axis_size("sub")
    return assemble(place, (near, second), third, modes, rows), two, beside, phi


def without(at, meta, by, room):
    kept = jnp.concatenate([meta[: at.start], jnp.full((at.start,), at.blocks_per, jnp.int32)])
    order = lax.dynamic_slice_in_dim(kept, by, at.start, 0)
    return jnp.concatenate([order, jnp.clip(meta[at.start :] - by, 0, room)])


def columns(part, modes, rows, groups):
    part = part[:, :rows, : groups * 4 * modes].astype(jnp.float32)
    part = part.reshape(*part.shape[:2], groups, 2, 2, modes).transpose(3, 1, 0, 4, 2, 5)
    return part.reshape(2, *part.shape[1:3], 2 * groups * modes)


def add_kernel(old, new, out):
    out[...] = old[...] + new[...]


def added(old, new):
    rows, owners, cols = old.shape
    block = pl.BlockSpec((rows, min(owners, 8), cols), lambda d: (0, d, 0))
    return pl.pallas_call(
        add_kernel,
        out_shape=jax.ShapeDtypeStruct(old.shape, old.dtype),
        grid=(owners // min(owners, 8),),
        in_specs=[block, block],
        out_specs=block,
        input_output_aliases={0: 0},
        compiler_params=pltpu.CompilerParams(vmem_limit_bytes=32 * MIB),
    )(old, new)


def per_device(phi, psi, k_blocks, m_blocks, block_row, block_col, live):
    count, modes, width = phi.shape
    at = Meta(count, k_blocks.shape[1], width // EDGE)
    blocks = (k_blocks, m_blocks)
    ints = (live, block_row, block_col)
    border = moved(psi[count - 1], "sub", 1)
    (whole,) = listed(at, 0, block_col, live)
    phi_whole, places = listed(at, 1, block_row, live, with_places=True)
    total = at.start + count + 1
    most = lax.pmax(jnp.stack([whole[total], phi_whole[total]]), "sub")
    over = jnp.maximum(most - jnp.asarray([ROOM, PHI_ROOM], jnp.int32), 0)
    each = jnp.asarray([MORE, PHI_ROOM], jnp.int32)
    trips = jnp.max((over + each - 1) // each)
    meta = jnp.concatenate([whole[: at.start], jnp.minimum(whole[at.start :], ROOM)])
    lists = (meta, phi_whole, places, trips)
    grids, far, trips, phi = main_path(at, lists, ints, phi, psi, border, blocks)

    def turned(whole):
        return whole.transpose(1, 0, 2)

    def more(state):
        n, phi, psi, far, before = state[0], state[1], state[2], state[3], state[4:]
        phi, psi, far = lax.optimization_barrier((phi, psi, far))
        phi, psi = turned(phi), turned(psi)

        rest = without(at, whole, ROOM + n * MORE, MORE)
        packed = pack(at, 0, MORE, rest, psi, border)
        packed = jnp.stack([packed] * lax.axis_size("grp"))
        packed = lax.all_to_all(packed, "grp", split_axis=0, concat_axis=0, tiled=True)
        coupling = couple(at, MORE, rest, *ints, [phi], *blocks)
        shards = [(packed[h],) for h in range(packed.shape[0])]
        part = to_owners(project(at, rest, [coupling], shards)[0], modes)
        after = columns(part, modes, grids[0].shape[0], len(shards))

        skipped = (n + 1) * PHI_ROOM
        rest = without(at, phi_whole, skipped, PHI_ROOM)
        phi_in = sent_in(pack(at, 0, PHI_ROOM, rest, phi))
        end = couple_end(at, meta, ints, places - skipped, phi_in, blocks)
        (part,) = project(at, meta, [end], [far])
        part = columns(to_owners(sent_back(part), modes), modes, grids[0].shape[0], 1)
        place, zero = lax.axis_index("grp"), jnp.zeros_like(part[..., :modes])
        last = lax.axis_size("grp") - 1
        ends = []
        for low in (0, modes):
            one = part[..., low : low + modes]
            for h in range(last + 1):
                wanted = ((place == 0) & (h == last)) | ((place == last) & (h == 0))
                ends.append(jnp.where(wanted, one, zero))
        after = after + jnp.concatenate(ends, axis=-1)
        return (n + 1, *state[1:4], *(added(old, new) for old, new in zip(before, after)))

    state = (jnp.int32(0), turned(phi), turned(psi), far, *grids)
    state = lax.while_loop(lambda state: state[0] < trips, more, state)
    return tuple(turned(grid)[None, None] for grid in state[4:])


def solution(mesh):
    placed = (
        P("sub", "grp", None),
        P("sub", "grp", None),
        P("sub", None, None, None),
        P("sub", None, None, None),
        P("sub", None),
        P("sub", None),
        P("sub"),
    )
    return jax.shard_map(
        per_device,
        mesh=mesh,
        in_specs=placed,
        out_specs=(P("sub", "grp", None, None, None), P("sub", "grp", None, None, None)),
        check_vma=False,
    )
```

profile of v0, /device:TPU:0, one launch (start us, length us, event | category | flops | bytes accessed | tf_op | source)
XLA Modules:
  0.0 204.8 jit_solution(6152013917558440178)
XLA Ops:
  0.7 3.7 %copy.51.refs_1_ = bf16[8,100,2048]{2,1,0:T(8,128)(2,1)S(1)} copy(bf16[8,100,2048]{2,0,1:T(8,128)(2,1)} %param.12) | data formatting | bytes 6553600 | tf_op args[1]
  5.3 3.1 %collective-permute-start.3 = (bf16[100,2048]{1,0:T(8,128)(2,1)}, bf16[100,2048]{1,0:T(8,128)(2,1)}, u32[]{:S(2)}, u32[]{:S(2)}) collective-permute-start(bf16[100,2048]{1,0:T(8,128)(2,1)} %slice_bitcast_fusion.6), channel_id=1, source_target_pairs={{0,4},{4,8},{8,12},{12,16},{16,20},{20,24},{24,28},{1,5},{5,9},{9,... | collective-permute-start | bytes 1228808 | tf_op jit(solution)/shard_map/ppermute | solution.py:403
  8.4 2.3 %shard_map.104 = s32[338]{0:T(512)S(1)} custom-call(s32[8]{0:T(128)S(1)} %copy-done.15, s32[8,24]{1,0:T(8,128)S(1)} %copy-done.13), custom_call_target="tpu_custom_call" | custom-call | flops 1 | bytes 1 | tf_op jit(solution)/shard_map/pallas_call | solution.py:88
  10.8 3.6 %shard_map.105.refs_1_ = bf16[100,12032]{1,0:T(8,128)(2,1)S(1)} custom-call(s32[338]{0:T(512)S(1)} %pad_add_fusion.2.meta, bf16[100,2048]{1,0:T(8,128)(2,1)} %collective-permute-done.3.refs_0_, bf16[8,100,2048]{2,1,0:T(8,128)(2,1)} %copy-done.5), custom_call_target="tpu_custom_call" | custom-call | flops 1 | bytes 1 | tf_op jit(solution)/shard_map/pallas_call | solution.py:120
  15.7 6.4 %collective-permute-start.4 = (bf16[100,12032]{1,0:T(8,128)(2,1)S(1)}, bf16[100,12032]{1,0:T(8,128)(2,1)}, u32[]{:S(2)}, u32[]{:S(2)}) collective-permute-start(bf16[100,12032]{1,0:T(8,128)(2,1)S(1)} %shard_map.105.refs_1_), channel_id=1, source_target_pairs={{0,1},{1,2},{2,3},{4,5},{5,6},{6,7},{8,9},{9,10},{10,11},{12,13},{... | collective-permute-start | bytes 7219208 | tf_op jit(solution)/shard_map/ppermute | solution.py:403
  22.1 3.4 %shard_map.106 = (s32[338]{0:T(512)S(1)}, s32[8,24]{1,0:T(8,128)S(1)}) custom-call(s32[8]{0:T(128)S(1)} %copy-done.15, s32[8,24]{1,0:T(8,128)S(1)} %copy-done.12), custom_call_target="tpu_custom_call" | custom-call | flops 1 | bytes 1 | tf_op jit(solution)/shard_map/pallas_call | solution.py:88
  25.5 3.7 %copy.50.refs_0_ = bf16[8,100,2048]{2,1,0:T(8,128)(2,1)S(1)} copy(bf16[8,100,2048]{2,0,1:T(8,128)(2,1)} %param.11) | data formatting | bytes 6553600 | tf_op jit(solution)/shard_map/optimization_barrier | solution.py:447
  29.3 3.5 %shard_map.109 = bf16[100,11776]{1,0:T(8,128)(2,1)} custom-call(s32[338]{0:T(512)S(1)} %get-tuple-element.474.meta, bf16[8,100,2048]{2,1,0:T(8,128)(2,1)S(1)} %copy.50.refs_0_), custom_call_target="tpu_custom_call" | custom-call | flops 1 | bytes 1 | tf_op jit(solution)/shard_map/pallas_call | solution.py:120
  32.7 2.1 %collective-permute-start.9 = (bf16[100,11776]{1,0:T(8,128)(2,1)}, bf16[100,11776]{1,0:T(8,128)(2,1)}, u32[]{:S(2)}, u32[]{:S(2)}) collective-permute-start(bf16[100,11776]{1,0:T(8,128)(2,1)} %shard_map.109), channel_id=1, source_target_pairs={{3,2},{7,6},{11,10},{15,14},{19,18},{23,22},{27,26},{31,30}} | collective-permute-start | bytes 7065608 | tf_op jit(solution)/shard_map/ppermute | solution.py:403
  34.8 3.9 %collective-permute-start.8 = (bf16[100,11776]{1,0:T(8,128)(2,1)}, bf16[100,11776]{1,0:T(8,128)(2,1)}, u32[]{:S(2)}, u32[]{:S(2)}) collective-permute-start(bf16[100,11776]{1,0:T(8,128)(2,1)} %shard_map.109), channel_id=1, source_target_pairs={{0,1},{4,5},{8,9},{12,13},{16,17},{20,21},{24,25},{28,29}} | collective-permute-start | bytes 7065608 | tf_op jit(solution)/shard_map/ppermute | solution.py:403
  41.2 12.9 %pmax.7 = s32[2]{0:T(128)S(1)} all-reduce(s32[2]{0:T(128)S(1)} %pad_add_fusion.4), channel_id=1, replica_groups=mesh['sub'=8,'grp'=4] {'sub'}, use_global_device_ids=true, to_apply=%region_0.0 | all-reduce | flops 2 | bytes 16 | tf_op jit(solution)/shard_map/pmax | solution.py:511
  55.0 17.5 %shard_map.107.refs_0_ = bf16[448,12032]{1,0:T(8,128)(2,1)} custom-call(s32[338]{0:T(512)S(1)} %pad_add_fusion.2.meta, s32[8]{0:T(128)S(1)} %copy-done.15, s32[8,24]{1,0:T(8,128)S(1)} %copy-done.12, s32[8,24]{1,0:T(8,128)S(1)} %copy-done.13, bf16[8,100,2048]{2,1,0:T(8,128)(2,1)} %copy-done.2, bf16[8,24,128,128]{3,2,1,0:T(8,128)(2,1)} %refs_2_.3, ...), custom_call_target="tpu_custom_call" | custom-call | flops 1 | bytes 1 | tf_op jit(solution)/shard_map/pallas_call | solution.py:187
  74.6 17.4 %shard_map.108 = bf16[8,104,1280]{2,1,0:T(8,128)(2,1)} custom-call(s32[338]{0:T(512)S(1)} %pad_add_fusion.2.meta, s32[1]{0:T(128)} %bitcast.19.me, bf16[448,12032]{1,0:T(8,128)(2,1)} %shard_map.107.refs_0_, bf16[100,12032]{1,0:T(8,128)(2,1)} %copy-done, bf16[100,12032]{1,0:T(8,128)(2,1)} %collective-permute-done.4.refs_2_, ...), custom_call_target="tpu_custom_call" | custom-call | flops 1 | bytes 1 | tf_op jit(solution)/shard_map/pallas_call | solution.py:313
  92.1 12.8 %all-to-all-start.3 = ((bf16[8,104,1280]{2,1,0:T(8,128)(2,1)}), bf16[8,104,1280]{2,1,0:T(8,128)(2,1)}, u32[]{:S(2)}, u32[]{:S(2)}) async-start(bf16[8,104,1280]{2,1,0:T(8,128)(2,1)} %shard_map.108), calls=%async_computation.3 | async-start | bytes 4259840 | tf_op jit(solution)/shard_map/all_to_all | solution.py:411
  104.9 19.8 %collective-permute-done.8 = bf16[100,11776]{1,0:T(8,128)(2,1)} collective-permute-done((bf16[100,11776]{1,0:T(8,128)(2,1)}, bf16[100,11776]{1,0:T(8,128)(2,1)}, u32[]{:S(2)}, u32[]{:S(2)}) %collective-permute-start.8) | collective-permute-done | bytes 2355232 | tf_op jit(solution)/shard_map/ppermute | solution.py:403
  124.7 18.4 %shard_map.110.refs_1_ = bf16[448,12032]{1,0:T(8,128)(2,1)} custom-call(s32[338]{0:T(512)S(1)} %pad_add_fusion.2.meta, s32[8]{0:T(128)S(1)} %copy-done.15, s32[8,24]{1,0:T(8,128)S(1)} %get-tuple-element.698.row, s32[8,24]{1,0:T(8,128)S(1)} %copy-done.13, bf16[1,100,11776]{2,1,0:T(8,128)(2,1)} %bitcast.21.refs_0_, bf16[1,100,11776]{2,1,0:T(8,128)(2,1)} %bitcast.22.refs_1_, ...), custom_call_target="tpu_custom_call" | custom-call | flops 24999999488 | bytes 1 | tf_op jit(solution)/shard_map/pallas_call | solution.py:187
  144.5 18.2 %shard_map.111 = (bf16[8,104,512]{2,1,0:T(8,128)(2,1)}, bf16[104,512]{1,0:T(8,128)(2,1)}, bf16[104,512]{1,0:T(8,128)(2,1)}, bf16[104,512]{1,0:T(8,128)(2,1)}, bf...) custom-call(s32[338]{0:T(512)S(1)} %pad_add_fusion.2.meta, ...), custom_call_target="tpu_custom_call" | custom-call | flops 1 | bytes 1 | tf_op jit(solution)/shard_map/pallas_call | solution.py:313
  162.7 8.6 %all-to-all-start.4 = ((bf16[8,104,512]{2,1,0:T(8,128)(2,1)}), bf16[8,104,512]{2,1,0:T(8,128)(2,1)}, u32[]{:S(2)}, u32[]{:S(2)}) async-start(bf16[8,104,512]{2,1,0:T(8,128)(2,1)} %get-tuple-element.479), calls=%async_computation.4 | async-start | bytes 1703936 | tf_op jit(solution)/shard_map/all_to_all | solution.py:411
  177.8 1.4 collective-permute-done.10.refs_0_
  179.3 1.5 collective-permute-start.15
  182.3 3.4 %collective-permute-done.12.refs_2_ = bf16[104,512]{1,0:T(8,128)(2,1)} collective-permute-done((bf16[104,512]{1,0:T(8,128)(2,1)}, bf16[104,512]{1,0:T(8,128)(2,1)}, u32[]{:S(2)}, u32[]{:S(2)}) %collective-permute-start.12) | collective-permute-done | bytes 106528 | tf_op jit(solution)/shard_map/ppermute | solution.py:432
  187.6 3.5 %collective-permute-done.14.refs_4_ = bf16[104,512]{1,0:T(8,128)(2,1)} collective-permute-done((bf16[104,512]{1,0:T(8,128)(2,1)}, bf16[104,512]{1,0:T(8,128)(2,1)}, u32[]{:S(2)}, u32[]{:S(2)}) %collective-permute-start.14) | collective-permute-done | bytes 106528 | tf_op jit(solution)/shard_map/ppermute | solution.py:432
  192.2 3.5 %collective-permute-done.16.refs_6_ = bf16[104,512]{1,0:T(8,128)(2,1)} collective-permute-done((bf16[104,512]{1,0:T(8,128)(2,1)}, bf16[104,512]{1,0:T(8,128)(2,1)}, u32[]{:S(2)}, u32[]{:S(2)}) %collective-permute-start.16) | collective-permute-done | bytes 106528 | tf_op jit(solution)/shard_map/ppermute | solution.py:432
  196.7 7.3 %shard_map.112 = (f32[100,8,800]{2,1,0:T(8,128)}, f32[100,8,800]{2,1,0:T(8,128)}) custom-call(s32[2]{0:T(128)} %pad_add_fusion.3.place, bf16[8,104,1280]{2,1,0:T(8,128)(2,1)} %all-to-all-done.3.near, bf16[8,104,512]{2,1,0:T(8,128)(2,1)} %all-to-all-done.4.second, bf16[104,512]{1,0:T(8,128)(2,1)} %copy-done.14, ...), custom_call_target="tpu_custom_call" | custom-call | flops 1 | bytes 1 | tf_op jit(solution)/shard_map/pallas_call | solution.py:381
  (53 shorter events, 21.9 us)
Async XLA Ops:
  0.6 7.7 %copy-start.15 = (s32[8]{0:T(128)S(1)}, s32[8]{0:T(128)}, u32[]{:S(2)}) copy-start(s32[8]{0:T(128)} %live.7) | copy-start | bytes 100
  5.3 5.6 %collective-permute-start.3 = (bf16[100,2048]{1,0:T(8,128)(2,1)}, bf16[100,2048]{1,0:T(8,128)(2,1)}, u32[]{:S(2)}, u32[]{:S(2)}) collective-permute-start(bf16[100,2048]{1,0:T(8,128)(2,1)} %slice_bitcast_fusion.6), channel_id=1, source_target_pairs={{0,4},{4,8},{8,12},{12,16},{16,20},{20,24},{24,28},{1,5},{5,9},{9,... | collective-permute-start | bytes 1228808 | tf_op jit(solution)/shard_map/ppermute | solution.py:403
  10.8 11.3 %copy-start.12 = (s32[8,24]{1,0:T(8,128)S(1)}, s32[8,24]{1,0:T(8,128)}, u32[]{:S(2)}) copy-start(s32[8,24]{1,0:T(8,128)} %row.1) | copy-start | bytes 2308
  14.4 14.8 %copy-start = (bf16[100,12032]{1,0:T(8,128)(2,1)}, bf16[100,12032]{1,0:T(8,128)(2,1)S(1)}, u32[]{:S(2)}) copy-start(bf16[100,12032]{1,0:T(8,128)(2,1)S(1)} %shard_map.105.refs_1_) | copy-start | bytes 7219204
  14.4 58.1 %collective-permute-start.5 = (bf16[100,12032]{1,0:T(8,128)(2,1)S(1)}, bf16[100,12032]{1,0:T(8,128)(2,1)}, u32[]{:S(2)}, u32[]{:S(2)}) collective-permute-start(bf16[100,12032]{1,0:T(8,128)(2,1)S(1)} %shard_map.105.refs_1_), channel_id=1, source_target_pairs={{1,0},{2,1},{3,2},{5,4},{6,5},{7,6},{9,8},{10,9},{11,10},{13,12},{... | collective-permute-start | bytes 7219208 | tf_op jit(solution)/shard_map/ppermute | solution.py:403
  15.7 56.8 %collective-permute-start.4 = (bf16[100,12032]{1,0:T(8,128)(2,1)S(1)}, bf16[100,12032]{1,0:T(8,128)(2,1)}, u32[]{:S(2)}, u32[]{:S(2)}) collective-permute-start(bf16[100,12032]{1,0:T(8,128)(2,1)S(1)} %shard_map.105.refs_1_), channel_id=1, source_target_pairs={{0,1},{1,2},{2,3},{4,5},{5,6},{6,7},{8,9},{9,10},{10,11},{12,13},{... | collective-permute-start | bytes 7219208 | tf_op jit(solution)/shard_map/ppermute | solution.py:403
  29.3 24.9 %copy-start.16 = (s32[2]{0:T(128)S(1)}, s32[2]{0:T(128)}, u32[]{:S(2)}) copy-start(s32[2]{0:T(128)} %constant.121) | copy-start | bytes 28
  29.3 24.9 %copy-start.17 = (s32[2]{0:T(128)S(1)}, s32[2]{0:T(128)}, u32[]{:S(2)}) copy-start(s32[2]{0:T(128)} %constant.116.clone) | copy-start | bytes 28
  32.7 72.2 %collective-permute-start.9 = (bf16[100,11776]{1,0:T(8,128)(2,1)}, bf16[100,11776]{1,0:T(8,128)(2,1)}, u32[]{:S(2)}, u32[]{:S(2)}) collective-permute-start(bf16[100,11776]{1,0:T(8,128)(2,1)} %shard_map.109), channel_id=1, source_target_pairs={{3,2},{7,6},{11,10},{15,14},{19,18},{23,22},{27,26},{31,30}} | collective-permute-start | bytes 7065608 | tf_op jit(solution)/shard_map/ppermute | solution.py:403
  34.8 89.9 %collective-permute-start.8 = (bf16[100,11776]{1,0:T(8,128)(2,1)}, bf16[100,11776]{1,0:T(8,128)(2,1)}, u32[]{:S(2)}, u32[]{:S(2)}) collective-permute-start(bf16[100,11776]{1,0:T(8,128)(2,1)} %shard_map.109), channel_id=1, source_target_pairs={{0,1},{4,5},{8,9},{12,13},{16,17},{20,21},{24,25},{28,29}} | collective-permute-start | bytes 7065608 | tf_op jit(solution)/shard_map/ppermute | solution.py:403
  72.5 70.6 %collective-permute-start.6 = (bf16[100,12032]{1,0:T(8,128)(2,1)}, bf16[100,12032]{1,0:T(8,128)(2,1)S(1)}, u32[]{:S(2)}, u32[]{:S(2)}) collective-permute-start(bf16[100,12032]{1,0:T(8,128)(2,1)} %collective-permute-done.4.refs_2_), channel_id=1, source_target_pairs={{1,2},{2,3},{5,6},{6,7},{9,10},{10,11},{13,14},{14,15},{17,18},{18... | collective-permute-start | bytes 7219208 | tf_op jit(solution)/shard_map/ppermute | solution.py:403
  73.3 69.8 %collective-permute-start.7 = (bf16[100,12032]{1,0:T(8,128)(2,1)}, bf16[100,12032]{1,0:T(8,128)(2,1)}, u32[]{:S(2)}, u32[]{:S(2)}) collective-permute-start(bf16[100,12032]{1,0:T(8,128)(2,1)} %collective-permute-done.5.refs_3_), channel_id=1, source_target_pairs={{2,1},{1,0},{6,5},{5,4},{10,9},{9,8},{14,13},{13,12},{18,17},{17,1... | collective-permute-start | bytes 7219208 | tf_op jit(solution)/shard_map/ppermute | solution.py:403
  92.1 51.0 %all-to-all-start.3 = ((bf16[8,104,1280]{2,1,0:T(8,128)(2,1)}), bf16[8,104,1280]{2,1,0:T(8,128)(2,1)}, u32[]{:S(2)}, u32[]{:S(2)}) async-start(bf16[8,104,1280]{2,1,0:T(8,128)(2,1)} %shard_map.108), calls=%async_computation.3 | async-start | bytes 4259840 | tf_op jit(solution)/shard_map/all_to_all | solution.py:411
  162.7 41.3 %copy-start.3 = (bf16[8,100,2048]{2,1,0:T(8,128)(2,1)S(1)}, bf16[8,100,2048]{2,1,0:T(8,128)(2,1)}, u32[]{:S(2)}) copy-start(bf16[8,100,2048]{2,1,0:T(8,128)(2,1)} %copy-done.2) | copy-start | bytes 9830404
  162.7 34.0 %all-to-all-start.4 = ((bf16[8,104,512]{2,1,0:T(8,128)(2,1)}), bf16[8,104,512]{2,1,0:T(8,128)(2,1)}, u32[]{:S(2)}, u32[]{:S(2)}) async-start(bf16[8,104,512]{2,1,0:T(8,128)(2,1)} %get-tuple-element.479), calls=%async_computation.4 | async-start | bytes 1703936 | tf_op jit(solution)/shard_map/all_to_all | solution.py:411
  171.3 7.9 %collective-permute-start.10 = (bf16[104,512]{1,0:T(8,128)(2,1)}, bf16[104,512]{1,0:T(8,128)(2,1)S(1)}, u32[]{:S(2)}, u32[]{:S(2)}) collective-permute-start(bf16[104,512]{1,0:T(8,128)(2,1)} %get-tuple-element.480), channel_id=1, source_target_pairs={{1,0},{5,4},{9,8},{13,12},{17,16},{21,20},{25,24},{29,28},{2,3},{6... | collective-permute-start | bytes 319496 | tf_op jit(solution)/shard_map/ppermute | solution.py:432
  172.6 8.4 %collective-permute-start.11 = (bf16[104,512]{1,0:T(8,128)(2,1)}, bf16[104,512]{1,0:T(8,128)(2,1)}, u32[]{:S(2)}, u32[]{:S(2)}) collective-permute-start(bf16[104,512]{1,0:T(8,128)(2,1)} %get-tuple-element.481), channel_id=1, source_target_pairs={{1,4},{5,0},{9,12},{13,8},{17,20},{21,16},{25,28},{29,24},{2,7},{6... | collective-permute-start | bytes 319496 | tf_op jit(solution)/shard_map/ppermute | solution.py:432
  173.9 11.8 %collective-permute-start.12 = (bf16[104,512]{1,0:T(8,128)(2,1)}, bf16[104,512]{1,0:T(8,128)(2,1)}, u32[]{:S(2)}, u32[]{:S(2)}) collective-permute-start(bf16[104,512]{1,0:T(8,128)(2,1)} %get-tuple-element.482), channel_id=1, source_target_pairs={{1,8},{5,12},{9,0},{13,4},{17,24},{21,28},{25,16},{29,20},{2,11},{... | collective-permute-start | bytes 319496 | tf_op jit(solution)/shard_map/ppermute | solution.py:432
  175.2 12.4 %collective-permute-start.13 = (bf16[104,512]{1,0:T(8,128)(2,1)}, bf16[104,512]{1,0:T(8,128)(2,1)}, u32[]{:S(2)}, u32[]{:S(2)}) collective-permute-start(bf16[104,512]{1,0:T(8,128)(2,1)} %get-tuple-element.483), channel_id=1, source_target_pairs={{1,12},{5,8},{9,4},{13,0},{17,28},{21,24},{25,20},{29,16},{2,15},{... | collective-permute-start | bytes 319496 | tf_op jit(solution)/shard_map/ppermute | solution.py:432
  176.5 14.6 %collective-permute-start.14 = (bf16[104,512]{1,0:T(8,128)(2,1)}, bf16[104,512]{1,0:T(8,128)(2,1)}, u32[]{:S(2)}, u32[]{:S(2)}) collective-permute-start(bf16[104,512]{1,0:T(8,128)(2,1)} %get-tuple-element.484), channel_id=1, source_target_pairs={{1,16},{5,20},{9,24},{13,28},{17,0},{21,4},{25,8},{29,12},{2,19},{... | collective-permute-start | bytes 319496 | tf_op jit(solution)/shard_map/ppermute | solution.py:432
  179.3 17.4 %copy-start.14 = (bf16[104,512]{1,0:T(8,128)(2,1)}, bf16[104,512]{1,0:T(8,128)(2,1)S(1)}, u32[]{:S(2)}) copy-start(bf16[104,512]{1,0:T(8,128)(2,1)S(1)} %collective-permute-done.10.refs_0_) | copy-start | bytes 319492
  179.3 13.0 %collective-permute-start.15 = (bf16[104,512]{1,0:T(8,128)(2,1)}, bf16[104,512]{1,0:T(8,128)(2,1)}, u32[]{:S(2)}, u32[]{:S(2)}) collective-permute-start(bf16[104,512]{1,0:T(8,128)(2,1)} %get-tuple-element.485), channel_id=1, source_target_pairs={{1,20},{5,16},{9,28},{13,24},{17,4},{21,0},{25,12},{29,8},{2,23},{... | collective-permute-start | bytes 319496 | tf_op jit(solution)/shard_map/ppermute | solution.py:432
  181.0 14.7 %collective-permute-start.16 = (bf16[104,512]{1,0:T(8,128)(2,1)}, bf16[104,512]{1,0:T(8,128)(2,1)}, u32[]{:S(2)}, u32[]{:S(2)}) collective-permute-start(bf16[104,512]{1,0:T(8,128)(2,1)} %get-tuple-element.486), channel_id=1, source_target_pairs={{1,24},{5,28},{9,16},{13,20},{17,8},{21,12},{25,0},{29,4},{2,27},{... | collective-permute-start | bytes 319496 | tf_op jit(solution)/shard_map/ppermute | solution.py:432
  185.7 11.0 %collective-permute-start.17 = (bf16[104,512]{1,0:T(8,128)(2,1)}, bf16[104,512]{1,0:T(8,128)(2,1)}, u32[]{:S(2)}, u32[]{:S(2)}) collective-permute-start(bf16[104,512]{1,0:T(8,128)(2,1)} %get-tuple-element.487), channel_id=1, source_target_pairs={{1,28},{5,24},{9,20},{13,16},{17,12},{21,8},{25,4},{29,0},{2,31},{... | collective-permute-start | bytes 319496 | tf_op jit(solution)/shard_map/ppermute | solution.py:432
  (4 other events, 19.1 us)
where the time goes:
time: 206 us; the launch traced here: 205 us
  Pallas kernels  91.5 us (44%)
  starting transfers between devices  50.8 us (25%)
  waiting for transfers between devices  34 us (17%)
  blocking collectives  12.9 us (6%)
  local copies, waits for them, and re-layouts  11 us (5%)
  other arithmetic  2.84 us (1%)
    pallas_call x2, Pallas kernels, couple(): pl.pallas_call(functools.partial(coupling_kernel, at, room, len(phis)), o...  35.9 us
    pallas_call x2, Pallas kernels, project(): pl.pallas_call(functools.partial(project_kernel, at, room, sets, many, sp...  35.6 us
    all_to_all x2, starting transfers between devices, to_owners(): return lax.all_to_all(part, 'sub', split_axis=0, concat_axis=0, tiled=True)  21.5 us
    ppermute x7, waiting for transfers between devices, moved(): return lax.ppermute(shard, axis, pairs)  19.8 us
    ppermute x7, starting transfers between devices, moved(): return lax.ppermute(shard, axis, pairs)  18.9 us
    ppermute x8, waiting for transfers between devices, sent_to_owners(): moved_to.append(lax.ppermute(part, ('sub', 'grp'), pairs))  14.2 us
    pmax x1, blocking collectives, per_device(): most = lax.pmax(jnp.stack([whole[total], phi_whole[total]]), 'sub')  12.9 us
    ppermute x8, starting transfers between devices, sent_to_owners(): moved_to.append(lax.ppermute(part, ('sub', 'grp'), pairs))  10.5 us
  transfers between devices with their start and end apart: 17, of which 8 were waited for; matrix products, arithmetic and copies ran while one was open for 4% of the time, Pallas kernels for 31%

commit v1 on v0

--- a/solution.py
+++ b/solution.py
@@ -12,7 +12,7 @@
 SLOTS = 8
 BITE = 4
 ROOM = 94
-PHI_ROOM = 92
+PHI_ROOM = 90
 MORE = 16
 MIB = 1 << 20
 LIGHT = pl.CostEstimate(flops=1, bytes_accessed=1, transcendentals=0)
@@ -273,7 +273,7 @@
     pieces = at.count if spread else 0
     outs, spreads, refs = refs[:many], refs[many - 1 : many - 1 + pieces], refs[many + max(pieces - 1, 0) :]
     helds, totals, (shard, right, held_done, shard_done) = refs[:many], refs[many : 2 * many], refs[2 * many :]
-    parts = [(0, room // 2), (room // 2, room)]
+    parts = [(0, room // 4), (room // 4, room)]
     coming = [[], []]
     for k, one in enumerate(shards):
         coming[0].append(pltpu.make_async_copy(one, shard.at[k], shard_done.at[k]))

time: 206 us -> 204 us (level)
  starting transfers between devices: 50.8 us -> 48.1 us
    all_to_all x2, starting transfers between devices: 21.5 us -> 18.8 us  [to_owners(): return lax.all_to_all(part, 'sub', split_axis=0, concat_axis=0, tiled=True)]
where the time goes in v1:
time: 204 us; the launch traced here: 203 us
  Pallas kernels  91.8 us (45%)
  starting transfers between devices  48.1 us (24%)
  waiting for transfers between devices  34.8 us (17%)
  blocking collectives  12.9 us (6%)
  local copies, waits for them, and re-layouts  11 us (5%)
  other arithmetic  2.75 us (1%)
    pallas_call x2, Pallas kernels, couple(): pl.pallas_call(functools.partial(coupling_kernel, at, room, len(phis)), o...  36 us
    pallas_call x2, Pallas kernels, project(): pl.pallas_call(functools.partial(project_kernel, at, room, sets, many, sp...  35.7 us
    ppermute x7, waiting for transfers between devices, moved(): return lax.ppermute(shard, axis, pairs)  20.3 us
    ppermute x7, starting transfers between devices, moved(): return lax.ppermute(shard, axis, pairs)  18.9 us
    all_to_all x2, starting transfers between devices, to_owners(): return lax.all_to_all(part, 'sub', split_axis=0, concat_axis=0, tiled=True)  18.8 us
    ppermute x8, waiting for transfers between devices, sent_to_owners(): moved_to.append(lax.ppermute(part, ('sub', 'grp'), pairs))  14.5 us
    pmax x1, blocking collectives, per_device(): most = lax.pmax(jnp.stack([whole[total], phi_whole[total]]), 'sub')  12.9 us
    ppermute x8, starting transfers between devices, sent_to_owners(): moved_to.append(lax.ppermute(part, ('sub', 'grp'), pairs))  10.5 us
  transfers between devices with their start and end apart: 17, of which 8 were waited for; matrix products, arithmetic and copies ran while one was open for 4% of the time, Pallas kernels for 31%

profile of v1, /device:TPU:0, one launch (start us, length us, event | category | flops | bytes accessed | tf_op | source)
XLA Modules:
  0.0 203.0 jit_solution(3478585838836195102)
XLA Ops:
  0.7 3.7 %copy.51.refs_1_ = bf16[8,100,2048]{2,1,0:T(8,128)(2,1)S(1)} copy(bf16[8,100,2048]{2,0,1:T(8,128)(2,1)} %param.12) | data formatting | bytes 6553600 | tf_op args[1]
  5.3 3.1 %collective-permute-start.3 = (bf16[100,2048]{1,0:T(8,128)(2,1)}, bf16[100,2048]{1,0:T(8,128)(2,1)}, u32[]{:S(2)}, u32[]{:S(2)}) collective-permute-start(bf16[100,2048]{1,0:T(8,128)(2,1)} %slice_bitcast_fusion.6), channel_id=1, source_target_pairs={{0,4},{4,8},{8,12},{12,16},{16,20},{20,24},{24,28},{1,5},{5,9},{9,... | collective-permute-start | bytes 1228808 | tf_op jit(solution)/shard_map/ppermute | solution.py:403
  8.4 2.3 %shard_map.104 = s32[334]{0:T(512)S(1)} custom-call(s32[8]{0:T(128)S(1)} %copy-done.15, s32[8,24]{1,0:T(8,128)S(1)} %copy-done.13), custom_call_target="tpu_custom_call" | custom-call | flops 1 | bytes 1 | tf_op jit(solution)/shard_map/pallas_call | solution.py:88
  10.8 3.7 %shard_map.105.refs_1_ = bf16[100,12032]{1,0:T(8,128)(2,1)S(1)} custom-call(s32[334]{0:T(512)S(1)} %pad_add_fusion.2.meta, bf16[100,2048]{1,0:T(8,128)(2,1)} %collective-permute-done.3.refs_0_, bf16[8,100,2048]{2,1,0:T(8,128)(2,1)} %copy-done.5), custom_call_target="tpu_custom_call" | custom-call | flops 1 | bytes 1 | tf_op jit(solution)/shard_map/pallas_call | solution.py:120
  15.8 6.4 %collective-permute-start.4 = (bf16[100,12032]{1,0:T(8,128)(2,1)S(1)}, bf16[100,12032]{1,0:T(8,128)(2,1)}, u32[]{:S(2)}, u32[]{:S(2)}) collective-permute-start(bf16[100,12032]{1,0:T(8,128)(2,1)S(1)} %shard_map.105.refs_1_), channel_id=1, source_target_pairs={{0,1},{1,2},{2,3},{4,5},{5,6},{6,7},{8,9},{9,10},{10,11},{12,13},{... | collective-permute-start | bytes 7219208 | tf_op jit(solution)/shard_map/ppermute | solution.py:403
  22.2 3.3 %shard_map.106 = (s32[334]{0:T(512)S(1)}, s32[8,24]{1,0:T(8,128)S(1)}) custom-call(s32[8]{0:T(128)S(1)} %copy-done.15, s32[8,24]{1,0:T(8,128)S(1)} %copy-done.12), custom_call_target="tpu_custom_call" | custom-call | flops 1 | bytes 1 | tf_op jit(solution)/shard_map/pallas_call | solution.py:88
  25.6 3.7 %copy.50.refs_0_ = bf16[8,100,2048]{2,1,0:T(8,128)(2,1)S(1)} copy(bf16[8,100,2048]{2,0,1:T(8,128)(2,1)} %param.11) | data formatting | bytes 6553600 | tf_op jit(solution)/shard_map/optimization_barrier | solution.py:447
  29.3 3.5 %shard_map.109 = bf16[100,11520]{1,0:T(8,128)(2,1)} custom-call(s32[334]{0:T(512)S(1)} %get-tuple-element.474.meta, bf16[8,100,2048]{2,1,0:T(8,128)(2,1)S(1)} %copy.50.refs_0_), custom_call_target="tpu_custom_call" | custom-call | flops 1 | bytes 1 | tf_op jit(solution)/shard_map/pallas_call | solution.py:120
  32.9 2.0 %collective-permute-start.9 = (bf16[100,11520]{1,0:T(8,128)(2,1)}, bf16[100,11520]{1,0:T(8,128)(2,1)}, u32[]{:S(2)}, u32[]{:S(2)}) collective-permute-start(bf16[100,11520]{1,0:T(8,128)(2,1)} %shard_map.109), channel_id=1, source_target_pairs={{3,2},{7,6},{11,10},{15,14},{19,18},{23,22},{27,26},{31,30}} | collective-permute-start | bytes 6912008 | tf_op jit(solution)/shard_map/ppermute | solution.py:403
  34.9 3.9 %collective-permute-start.8 = (bf16[100,11520]{1,0:T(8,128)(2,1)}, bf16[100,11520]{1,0:T(8,128)(2,1)}, u32[]{:S(2)}, u32[]{:S(2)}) collective-permute-start(bf16[100,11520]{1,0:T(8,128)(2,1)} %shard_map.109), channel_id=1, source_target_pairs={{0,1},{4,5},{8,9},{12,13},{16,17},{20,21},{24,25},{28,29}} | collective-permute-start | bytes 6912008 | tf_op jit(solution)/shard_map/ppermute | solution.py:403
  41.3 12.9 %pmax.7 = s32[2]{0:T(128)S(1)} all-reduce(s32[2]{0:T(128)S(1)} %pad_add_fusion.4), channel_id=1, replica_groups=mesh['sub'=8,'grp'=4] {'sub'}, use_global_device_ids=true, to_apply=%region_0.0 | all-reduce | flops 2 | bytes 16 | tf_op jit(solution)/shard_map/pmax | solution.py:511
  54.9 17.6 %shard_map.107.refs_0_ = bf16[448,12032]{1,0:T(8,128)(2,1)} custom-call(s32[334]{0:T(512)S(1)} %pad_add_fusion.2.meta, s32[8]{0:T(128)S(1)} %copy-done.15, s32[8,24]{1,0:T(8,128)S(1)} %copy-done.12, s32[8,24]{1,0:T(8,128)S(1)} %copy-done.13, bf16[8,100,2048]{2,1,0:T(8,128)(2,1)} %copy-done.2, bf16[8,24,128,128]{3,2,1,0:T(8,128)(2,1)} %refs_2_.3, ...), custom_call_target="tpu_custom_call" | custom-call | flops 1 | bytes 1 | tf_op jit(solution)/shard_map/pallas_call | solution.py:187
  74.7 17.5 %shard_map.108 = bf16[8,104,1280]{2,1,0:T(8,128)(2,1)} custom-call(s32[334]{0:T(512)S(1)} %pad_add_fusion.2.meta, s32[1]{0:T(128)} %bitcast.19.me, bf16[448,12032]{1,0:T(8,128)(2,1)} %shard_map.107.refs_0_, bf16[100,12032]{1,0:T(8,128)(2,1)} %copy-done, bf16[100,12032]{1,0:T(8,128)(2,1)} %collective-permute-done.4.refs_2_, ...), custom_call_target="tpu_custom_call" | custom-call | flops 1 | bytes 1 | tf_op jit(solution)/shard_map/pallas_call | solution.py:313
  92.2 11.1 %all-to-all-start.3 = ((bf16[8,104,1280]{2,1,0:T(8,128)(2,1)}), bf16[8,104,1280]{2,1,0:T(8,128)(2,1)}, u32[]{:S(2)}, u32[]{:S(2)}) async-start(bf16[8,104,1280]{2,1,0:T(8,128)(2,1)} %shard_map.108), calls=%async_computation.3 | async-start | bytes 4259840 | tf_op jit(solution)/shard_map/all_to_all | solution.py:411
  103.2 20.2 %collective-permute-done.8 = bf16[100,11520]{1,0:T(8,128)(2,1)} collective-permute-done((bf16[100,11520]{1,0:T(8,128)(2,1)}, bf16[100,11520]{1,0:T(8,128)(2,1)}, u32[]{:S(2)}, u32[]{:S(2)}) %collective-permute-start.8) | collective-permute-done | bytes 2304032 | tf_op jit(solution)/shard_map/ppermute | solution.py:403
  123.5 18.4 %shard_map.110.refs_1_ = bf16[448,12032]{1,0:T(8,128)(2,1)} custom-call(s32[334]{0:T(512)S(1)} %pad_add_fusion.2.meta, s32[8]{0:T(128)S(1)} %copy-done.15, s32[8,24]{1,0:T(8,128)S(1)} %get-tuple-element.698.row, s32[8,24]{1,0:T(8,128)S(1)} %copy-done.13, bf16[1,100,11520]{2,1,0:T(8,128)(2,1)} %bitcast.21.refs_0_, bf16[1,100,11520]{2,1,0:T(8,128)(2,1)} %bitcast.22.refs_1_, ...), custom_call_target="tpu_custom_call" | custom-call | flops 24999999488 | bytes 1 | tf_op jit(solution)/shard_map/pallas_call | solution.py:187
  143.4 18.2 %shard_map.111 = (bf16[8,104,512]{2,1,0:T(8,128)(2,1)}, bf16[104,512]{1,0:T(8,128)(2,1)}, bf16[104,512]{1,0:T(8,128)(2,1)}, bf16[104,512]{1,0:T(8,128)(2,1)}, bf...) custom-call(s32[334]{0:T(512)S(1)} %pad_add_fusion.2.meta, ...), custom_call_target="tpu_custom_call" | custom-call | flops 1 | bytes 1 | tf_op jit(solution)/shard_map/pallas_call | solution.py:313
  161.6 7.7 %all-to-all-start.4 = ((bf16[8,104,512]{2,1,0:T(8,128)(2,1)}), bf16[8,104,512]{2,1,0:T(8,128)(2,1)}, u32[]{:S(2)}, u32[]{:S(2)}) async-start(bf16[8,104,512]{2,1,0:T(8,128)(2,1)} %get-tuple-element.479), calls=%async_computation.4 | async-start | bytes 1703936 | tf_op jit(solution)/shard_map/all_to_all | solution.py:411
  177.6 1.8 collective-permute-done.11.refs_1_
  180.7 2.8 %collective-permute-done.12.refs_2_ = bf16[104,512]{1,0:T(8,128)(2,1)} collective-permute-done((bf16[104,512]{1,0:T(8,128)(2,1)}, bf16[104,512]{1,0:T(8,128)(2,1)}, u32[]{:S(2)}, u32[]{:S(2)}) %collective-permute-start.12) | collective-permute-done | bytes 106528 | tf_op jit(solution)/shard_map/ppermute | solution.py:432
  185.4 3.9 %collective-permute-done.14.refs_4_ = bf16[104,512]{1,0:T(8,128)(2,1)} collective-permute-done((bf16[104,512]{1,0:T(8,128)(2,1)}, bf16[104,512]{1,0:T(8,128)(2,1)}, u32[]{:S(2)}, u32[]{:S(2)}) %collective-permute-start.14) | collective-permute-done | bytes 106528 | tf_op jit(solution)/shard_map/ppermute | solution.py:432
  189.2 1.7 collective-permute-done.15.refs_5_
  191.0 3.0 %collective-permute-done.16.refs_6_ = bf16[104,512]{1,0:T(8,128)(2,1)} collective-permute-done((bf16[104,512]{1,0:T(8,128)(2,1)}, bf16[104,512]{1,0:T(8,128)(2,1)}, u32[]{:S(2)}, u32[]{:S(2)}) %collective-permute-start.16) | collective-permute-done | bytes 106528 | tf_op jit(solution)/shard_map/ppermute | solution.py:432
  195.0 7.3 %shard_map.112 = (f32[100,8,800]{2,1,0:T(8,128)}, f32[100,8,800]{2,1,0:T(8,128)}) custom-call(s32[2]{0:T(128)} %pad_add_fusion.3.place, bf16[8,104,1280]{2,1,0:T(8,128)(2,1)} %all-to-all-done.3.near, bf16[8,104,512]{2,1,0:T(8,128)(2,1)} %all-to-all-done.4.second, bf16[104,512]{1,0:T(8,128)(2,1)} %copy-done.14, ...), custom_call_target="tpu_custom_call" | custom-call | flops 1 | bytes 1 | tf_op jit(solution)/shard_map/pallas_call | solution.py:381
  (53 shorter events, 22.1 us)
Async XLA Ops:
  0.6 7.7 %copy-start.15 = (s32[8]{0:T(128)S(1)}, s32[8]{0:T(128)}, u32[]{:S(2)}) copy-start(s32[8]{0:T(128)} %live.7) | copy-start | bytes 100
  5.3 5.6 %collective-permute-start.3 = (bf16[100,2048]{1,0:T(8,128)(2,1)}, bf16[100,2048]{1,0:T(8,128)(2,1)}, u32[]{:S(2)}, u32[]{:S(2)}) collective-permute-start(bf16[100,2048]{1,0:T(8,128)(2,1)} %slice_bitcast_fusion.6), channel_id=1, source_target_pairs={{0,4},{4,8},{8,12},{12,16},{16,20},{20,24},{24,28},{1,5},{5,9},{9,... | collective-permute-start | bytes 1228808 | tf_op jit(solution)/shard_map/ppermute | solution.py:403
  10.8 11.4 %copy-start.12 = (s32[8,24]{1,0:T(8,128)S(1)}, s32[8,24]{1,0:T(8,128)}, u32[]{:S(2)}) copy-start(s32[8,24]{1,0:T(8,128)} %row.1) | copy-start | bytes 2308
  14.5 14.8 %copy-start = (bf16[100,12032]{1,0:T(8,128)(2,1)}, bf16[100,12032]{1,0:T(8,128)(2,1)S(1)}, u32[]{:S(2)}) copy-start(bf16[100,12032]{1,0:T(8,128)(2,1)S(1)} %shard_map.105.refs_1_) | copy-start | bytes 7219204
  14.5 58.0 %collective-permute-start.5 = (bf16[100,12032]{1,0:T(8,128)(2,1)S(1)}, bf16[100,12032]{1,0:T(8,128)(2,1)}, u32[]{:S(2)}, u32[]{:S(2)}) collective-permute-start(bf16[100,12032]{1,0:T(8,128)(2,1)S(1)} %shard_map.105.refs_1_), channel_id=1, source_target_pairs={{1,0},{2,1},{3,2},{5,4},{6,5},{7,6},{9,8},{10,9},{11,10},{13,12},{... | collective-permute-start | bytes 7219208 | tf_op jit(solution)/shard_map/ppermute | solution.py:403
  15.8 56.7 %collective-permute-start.4 = (bf16[100,12032]{1,0:T(8,128)(2,1)S(1)}, bf16[100,12032]{1,0:T(8,128)(2,1)}, u32[]{:S(2)}, u32[]{:S(2)}) collective-permute-start(bf16[100,12032]{1,0:T(8,128)(2,1)S(1)} %shard_map.105.refs_1_), channel_id=1, source_target_pairs={{0,1},{1,2},{2,3},{4,5},{5,6},{6,7},{8,9},{9,10},{10,11},{12,13},{... | collective-permute-start | bytes 7219208 | tf_op jit(solution)/shard_map/ppermute | solution.py:403
  29.3 24.9 %copy-start.16 = (s32[2]{0:T(128)S(1)}, s32[2]{0:T(128)}, u32[]{:S(2)}) copy-start(s32[2]{0:T(128)} %constant.121) | copy-start | bytes 28
  29.3 24.9 %copy-start.17 = (s32[2]{0:T(128)S(1)}, s32[2]{0:T(128)}, u32[]{:S(2)}) copy-start(s32[2]{0:T(128)} %constant.116.clone) | copy-start | bytes 28
  32.9 70.4 %collective-permute-start.9 = (bf16[100,11520]{1,0:T(8,128)(2,1)}, bf16[100,11520]{1,0:T(8,128)(2,1)}, u32[]{:S(2)}, u32[]{:S(2)}) collective-permute-start(bf16[100,11520]{1,0:T(8,128)(2,1)} %shard_map.109), channel_id=1, source_target_pairs={{3,2},{7,6},{11,10},{15,14},{19,18},{23,22},{27,26},{31,30}} | collective-permute-start | bytes 6912008 | tf_op jit(solution)/shard_map/ppermute | solution.py:403
  34.9 88.6 %collective-permute-start.8 = (bf16[100,11520]{1,0:T(8,128)(2,1)}, bf16[100,11520]{1,0:T(8,128)(2,1)}, u32[]{:S(2)}, u32[]{:S(2)}) collective-permute-start(bf16[100,11520]{1,0:T(8,128)(2,1)} %shard_map.109), channel_id=1, source_target_pairs={{0,1},{4,5},{8,9},{12,13},{16,17},{20,21},{24,25},{28,29}} | collective-permute-start | bytes 6912008 | tf_op jit(solution)/shard_map/ppermute | solution.py:403
  72.5 69.4 %collective-permute-start.6 = (bf16[100,12032]{1,0:T(8,128)(2,1)}, bf16[100,12032]{1,0:T(8,128)(2,1)S(1)}, u32[]{:S(2)}, u32[]{:S(2)}) collective-permute-start(bf16[100,12032]{1,0:T(8,128)(2,1)} %collective-permute-done.4.refs_2_), channel_id=1, source_target_pairs={{1,2},{2,3},{5,6},{6,7},{9,10},{10,11},{13,14},{14,15},{17,18},{18... | collective-permute-start | bytes 7219208 | tf_op jit(solution)/shard_map/ppermute | solution.py:403
  73.4 68.6 %collective-permute-start.7 = (bf16[100,12032]{1,0:T(8,128)(2,1)}, bf16[100,12032]{1,0:T(8,128)(2,1)}, u32[]{:S(2)}, u32[]{:S(2)}) collective-permute-start(bf16[100,12032]{1,0:T(8,128)(2,1)} %collective-permute-done.5.refs_3_), channel_id=1, source_target_pairs={{2,1},{1,0},{6,5},{5,4},{10,9},{9,8},{14,13},{13,12},{18,17},{17,1... | collective-permute-start | bytes 7219208 | tf_op jit(solution)/shard_map/ppermute | solution.py:403
  92.2 49.7 %all-to-all-start.3 = ((bf16[8,104,1280]{2,1,0:T(8,128)(2,1)}), bf16[8,104,1280]{2,1,0:T(8,128)(2,1)}, u32[]{:S(2)}, u32[]{:S(2)}) async-start(bf16[8,104,1280]{2,1,0:T(8,128)(2,1)} %shard_map.108), calls=%async_computation.3 | async-start | bytes 4259840 | tf_op jit(solution)/shard_map/all_to_all | solution.py:411
  161.6 40.7 %copy-start.3 = (bf16[8,100,2048]{2,1,0:T(8,128)(2,1)S(1)}, bf16[8,100,2048]{2,1,0:T(8,128)(2,1)}, u32[]{:S(2)}) copy-start(bf16[8,100,2048]{2,1,0:T(8,128)(2,1)} %copy-done.2) | copy-start | bytes 9830404
  161.6 33.4 %all-to-all-start.4 = ((bf16[8,104,512]{2,1,0:T(8,128)(2,1)}), bf16[8,104,512]{2,1,0:T(8,128)(2,1)}, u32[]{:S(2)}, u32[]{:S(2)}) async-start(bf16[8,104,512]{2,1,0:T(8,128)(2,1)} %get-tuple-element.479), calls=%async_computation.4 | async-start | bytes 1703936 | tf_op jit(solution)/shard_map/all_to_all | solution.py:411
  169.3 6.8 %collective-permute-start.10 = (bf16[104,512]{1,0:T(8,128)(2,1)}, bf16[104,512]{1,0:T(8,128)(2,1)S(1)}, u32[]{:S(2)}, u32[]{:S(2)}) collective-permute-start(bf16[104,512]{1,0:T(8,128)(2,1)} %get-tuple-element.480), channel_id=1, source_target_pairs={{1,0},{5,4},{9,8},{13,12},{17,16},{21,20},{25,24},{29,28},{2,3},{6... | collective-permute-start | bytes 319496 | tf_op jit(solution)/shard_map/ppermute | solution.py:432
  170.6 8.8 %collective-permute-start.11 = (bf16[104,512]{1,0:T(8,128)(2,1)}, bf16[104,512]{1,0:T(8,128)(2,1)}, u32[]{:S(2)}, u32[]{:S(2)}) collective-permute-start(bf16[104,512]{1,0:T(8,128)(2,1)} %get-tuple-element.481), channel_id=1, source_target_pairs={{1,4},{5,0},{9,12},{13,8},{17,20},{21,16},{25,28},{29,24},{2,7},{6... | collective-permute-start | bytes 319496 | tf_op jit(solution)/shard_map/ppermute | solution.py:432
  171.9 11.6 %collective-permute-start.12 = (bf16[104,512]{1,0:T(8,128)(2,1)}, bf16[104,512]{1,0:T(8,128)(2,1)}, u32[]{:S(2)}, u32[]{:S(2)}) collective-permute-start(bf16[104,512]{1,0:T(8,128)(2,1)} %get-tuple-element.482), channel_id=1, source_target_pairs={{1,8},{5,12},{9,0},{13,4},{17,24},{21,28},{25,16},{29,20},{2,11},{... | collective-permute-start | bytes 319496 | tf_op jit(solution)/shard_map/ppermute | solution.py:432
  173.2 12.2 %collective-permute-start.13 = (bf16[104,512]{1,0:T(8,128)(2,1)}, bf16[104,512]{1,0:T(8,128)(2,1)}, u32[]{:S(2)}, u32[]{:S(2)}) collective-permute-start(bf16[104,512]{1,0:T(8,128)(2,1)} %get-tuple-element.483), channel_id=1, source_target_pairs={{1,12},{5,8},{9,4},{13,0},{17,28},{21,24},{25,20},{29,16},{2,15},{... | collective-permute-start | bytes 319496 | tf_op jit(solution)/shard_map/ppermute | solution.py:432
  174.5 14.7 %collective-permute-start.14 = (bf16[104,512]{1,0:T(8,128)(2,1)}, bf16[104,512]{1,0:T(8,128)(2,1)}, u32[]{:S(2)}, u32[]{:S(2)}) collective-permute-start(bf16[104,512]{1,0:T(8,128)(2,1)} %get-tuple-element.484), channel_id=1, source_target_pairs={{1,16},{5,20},{9,24},{13,28},{17,0},{21,4},{25,8},{29,12},{2,19},{... | collective-permute-start | bytes 319496 | tf_op jit(solution)/shard_map/ppermute | solution.py:432
  176.1 18.9 %copy-start.14 = (bf16[104,512]{1,0:T(8,128)(2,1)}, bf16[104,512]{1,0:T(8,128)(2,1)S(1)}, u32[]{:S(2)}) copy-start(bf16[104,512]{1,0:T(8,128)(2,1)S(1)} %collective-permute-done.10.refs_0_) | copy-start | bytes 319492
  176.2 14.8 %collective-permute-start.15 = (bf16[104,512]{1,0:T(8,128)(2,1)}, bf16[104,512]{1,0:T(8,128)(2,1)}, u32[]{:S(2)}, u32[]{:S(2)}) collective-permute-start(bf16[104,512]{1,0:T(8,128)(2,1)} %get-tuple-element.485), channel_id=1, source_target_pairs={{1,20},{5,16},{9,28},{13,24},{17,4},{21,0},{25,12},{29,8},{2,23},{... | collective-permute-start | bytes 319496 | tf_op jit(solution)/shard_map/ppermute | solution.py:432
  179.4 14.6 %collective-permute-start.16 = (bf16[104,512]{1,0:T(8,128)(2,1)}, bf16[104,512]{1,0:T(8,128)(2,1)}, u32[]{:S(2)}, u32[]{:S(2)}) collective-permute-start(bf16[104,512]{1,0:T(8,128)(2,1)} %get-tuple-element.486), channel_id=1, source_target_pairs={{1,24},{5,28},{9,16},{13,20},{17,8},{21,12},{25,0},{29,4},{2,27},{... | collective-permute-start | bytes 319496 | tf_op jit(solution)/shard_map/ppermute | solution.py:432
  183.5 11.5 %collective-permute-start.17 = (bf16[104,512]{1,0:T(8,128)(2,1)}, bf16[104,512]{1,0:T(8,128)(2,1)}, u32[]{:S(2)}, u32[]{:S(2)}) collective-permute-start(bf16[104,512]{1,0:T(8,128)(2,1)} %get-tuple-element.487), channel_id=1, source_target_pairs={{1,28},{5,24},{9,20},{13,16},{17,12},{21,8},{25,4},{29,0},{2,31},{... | collective-permute-start | bytes 319496 | tf_op jit(solution)/shard_map/ppermute | solution.py:432
  (4 other events, 19.2 us)
